TPU v7x, 32 devices: a whole 2x2x4 slice. The times are simulated.
32 devices in a mesh: fiber: 2 (over x), chan: 16 (over z, y, core).
Axes of the slice: x: 2, y: 2, z: 4, core: 2. Of those that a mesh axis runs over, the one named last changes fastest.
Arguments:
- recording: bfloat16 [1024, 16384], P('fiber', 'chan'), parts along dimension 0, may hold values from -6 to 6
- source_index: int32 [1024], P('fiber'), parts along dimension 0, may hold values from 0 to 511
- channel_mask: int32 [1024], P(('fiber', 'chan')), parts along dimension 0, may hold values 0 or 1
Outputs:
- correlations: bfloat16 [1024, 512, 256], P('fiber', 'chan'), parts along dimension 0
There are 2 independent parts, one for each index of `fiber`. A program takes and returns all parts, laid end to end along the dimension named above; each array names one. Nothing has to cross between parts.
Inputs may be any that keep to these rules, and one draw needn't show every extreme that they name: `source_index`: indices of virtual-source channels of this fiber; they may repeat and may name bad channels. `channel_mask`: one flag for each channel.
All inputs are finite; a program needn't handle non-finite values. No bound on the sum of `channel_mask` on one device may be relied on, other than what follows from the above.
Results may differ from a plain program's by a relative error of at most 0.0092.
Values may be sent and summed in bfloat16 or wider, within the bound.
A program may use at most 128 MiB of HBM per device.

v0:
```python
import math

import jax
import jax.numpy as jnp
from jax import lax
from jax.sharding import PartitionSpec as P

SEGS = 8
NSEG = 512
NF = 192
FBASE = 4
LAGS = 256
TAPS = 64
SOURCES = 512


def from_behind(block, axis, distance):
    devices = range(lax.axis_size(axis))
    route = [(i - distance, i) for i in devices if i - distance in devices]
    return lax.ppermute(block, axis, route)


def lowpass_taps():
    offsets = jnp.arange(TAPS, dtype=jnp.float32) - (TAPS - 1) / 2.0
    cutoff = 0.1
    window = 0.5 - 0.5 * jnp.cos(2.0 * math.pi * (jnp.arange(TAPS, dtype=jnp.float32) + 0.5) / TAPS)
    kernel = 2.0 * cutoff * jnp.sinc(2.0 * cutoff * offsets) * window
    kernel = kernel / jnp.sum(kernel)
    return kernel[::-1].astype(jnp.bfloat16)


def decimate(padded, reversed_taps, out_length):
    summed = jnp.zeros((padded.shape[0], out_length), jnp.float32)
    for stride in range(TAPS // 4):
        window_rows = padded[:, 4 * stride : 4 * stride + 4 * out_length].reshape(
            padded.shape[0], out_length, 4
        )
        weights = reversed_taps[4 * stride : 4 * stride + 4]
        summed = summed + jnp.einsum(
            "ctq,q->ct", window_rows, weights, preferred_element_type=jnp.float32
        )
    return summed.astype(jnp.bfloat16)


def fourier_table():
    sample = jnp.arange(NSEG, dtype=jnp.int32)[:, None]
    frequency = FBASE + jnp.arange(NF, dtype=jnp.int32)[None, :]
    angles = 2.0 * math.pi * (sample * frequency % NSEG).astype(jnp.float32) / NSEG
    return jnp.concatenate([jnp.cos(angles), -jnp.sin(angles)], axis=1).astype(jnp.bfloat16)


def delay_table():
    frequency = FBASE + jnp.arange(NF, dtype=jnp.int32)[:, None]
    delays = jnp.arange(LAGS, dtype=jnp.int32)[None, :] - LAGS // 2
    angles = 2.0 * math.pi * (frequency * delays % NSEG).astype(jnp.float32) / NSEG
    return jnp.concatenate([jnp.cos(angles), -jnp.sin(angles)], axis=0).astype(jnp.bfloat16)


def whiten(spectrum):
    real_part = spectrum[:, :NF]
    imag_part = spectrum[:, NF:]
    power = real_part * real_part + imag_part * imag_part
    average = jnp.mean(power, axis=1, keepdims=True)
    factor = lax.rsqrt(power + 0.1 * average + 1e-05)
    return jnp.concatenate([real_part * factor, imag_part * factor], axis=1).astype(jnp.bfloat16)


def correlate(chosen, receivers, delays):
    source_real = chosen[..., :NF]
    source_imag = chosen[..., NF:]
    recv_real = receivers[..., :NF]
    recv_imag = receivers[..., NF:]
    cross_real = jnp.einsum(
        "swf,rwf->srf", source_real, recv_real, preferred_element_type=jnp.float32
    )
    cross_real = cross_real + jnp.einsum(
        "swf,rwf->srf", source_imag, recv_imag, preferred_element_type=jnp.float32
    )
    cross_imag = jnp.einsum(
        "swf,rwf->srf", source_imag, recv_real, preferred_element_type=jnp.float32
    )
    cross_imag = cross_imag - jnp.einsum(
        "swf,rwf->srf", source_real, recv_imag, preferred_element_type=jnp.float32
    )
    cross = jnp.concatenate([cross_real, cross_imag], axis=2).astype(jnp.bfloat16)
    source_count = chosen.shape[0]
    recv_count = receivers.shape[0]
    lagged = jnp.dot(
        cross.reshape(source_count * recv_count, 2 * NF), delays, preferred_element_type=jnp.float32
    )
    lagged = lagged.reshape(source_count, recv_count, LAGS) * (1.0 / math.sqrt(SEGS * NF))
    return lagged.astype(jnp.bfloat16)


def body(recording, source_index, channel_mask):
    channels, raw_count = recording.shape
    devices = lax.axis_size("chan")
    per_device = channels // devices
    dec_length = raw_count // 4
    trailing = recording[:, raw_count - (TAPS - 4) :]
    earlier = from_behind(trailing, "chan", 1)
    padded = jnp.concatenate([earlier, recording], axis=1)
    decimated = decimate(padded, lowpass_taps(), dec_length)
    grouped = decimated.reshape(devices, per_device, dec_length)
    fourier = fourier_table()
    block = lax.all_to_all(grouped, "chan", split_axis=0, concat_axis=2, tiled=True)
    members = block.shape[1]
    segments = block.reshape(members * SEGS, NSEG)
    spectrum = jnp.dot(segments, fourier, preferred_element_type=jnp.float32)
    whitened = whiten(spectrum).reshape(members, SEGS, 2 * NF)
    whitened = whitened * channel_mask.astype(jnp.bfloat16)[:, None, None]
    initial = jnp.zeros((SOURCES, SEGS, 2 * NF), jnp.bfloat16)
    shard_rows = lax.all_gather(whitened, "chan", axis=0, tiled=True)
    row_count = shard_rows.shape[0]
    inside = (source_index >= 0) & (source_index < row_count)
    picked_rows = jnp.take(shard_rows, jnp.clip(source_index, 0, row_count - 1), axis=0)
    chosen = jnp.where(inside[:, None, None], picked_rows, initial)
    delays = delay_table()

    def one_block(chosen_block):
        return correlate(chosen_block, whitened, delays)

    blocks = chosen.reshape(4, SOURCES // 4, SEGS, 2 * NF)
    result = lax.map(one_block, blocks)
    return result.reshape(SOURCES, per_device, LAGS)


def solution(mesh):
    placed = (P("fiber", "chan"), P("fiber"), P(("fiber", "chan")))
    return jax.shard_map(
        body, mesh=mesh, in_specs=placed, out_specs=P("fiber", "chan", None), check_vma=False
    )
```

profile of v0, /device:TPU:0, one launch (start us, length us, event | category | flops | bytes accessed | tf_op | source)
XLA Modules:
  0.0 241.6 jit_solution(927293739654847084)
XLA Ops:
  7.5 2.4 collective-permute-start
  10.6 1.5 copy.81
  15.2 5.0 %fusion.27 = (bf16[512,1024]{1,0:T(8,128)(2,1)}, bf16[512,1024]{1,0:T(8,128)(2,1)}, bf16[512,1024]{1,0:T(8,128)(2,1)}, bf16[512,1024]{1,0:T(8,128)(2,1)}, bf16[5...) fusion(bf16[512,60]{1,0:T(8,128)(2,1)S(1)} %collective-permute-, ...), kind=kLoop, calls=%fused_computation.46 | loop fusion | flops 18874368 | bytes 10547200 | tf_op jit(solution)/shard_map/concatenate | solution.py:102
  20.2 1.5 copy.66
  22.8 1.9 fusion.62
  24.7 1.2 copy.86
  25.9 1.5 copy.67
  28.5 2.0 fusion.63
  31.7 1.5 copy.68
  34.3 2.0 fusion.64
  36.3 1.2 copy.88
  37.5 1.5 copy.69
  40.1 2.0 fusion.65
  42.1 1.2 copy.89
  43.3 1.5 copy.70
  45.9 2.0 fusion.66
  49.0 1.5 copy.71
  51.7 2.0 fusion.67
  54.8 1.5 copy.72
  57.4 2.0 fusion.68
  60.6 1.5 copy.73
  63.2 2.0 fusion.69
  68.0 1.2 copy.94
  69.2 3.5 %fusion.36 = (bf16[512,1024]{1,0:T(8,128)(2,1)}, bf16[512,1024]{1,0:T(8,128)(2,1)}, bf16[512,1024]{1,0:T(8,128)(2,1)}, bf16[512,1024]{1,0:T(8,128)(2,1)S(1)}, bf...) fusion(bf16[512,60]{1,0:T(8,128)(2,1)S(1)} %collective-permute-done, bf16[512,1024]{1,0:T(8,128)(2,1)S(1)} %copy-done), kind=kLoop, calls=%fused_computation.55 | loop fusion | flops 12582912 | bytes 7401472 | tf_op jit(solution)/shard_map/concatenate | solution.py:102
  72.7 2.3 copy.80
  75.0 2.2 reshape.118
  77.2 2.8 %fusion.76 = f32[1,512,256]{1,0,2:T(1,128)} fusion(bf16[512,256,4]{0,2,1:T(4,128)(2,1)} %reshape.118, bf16[64]{0:T(256)(128)(2,1)S(1)} %divide_convert_fusion), kind=kOutput, calls=%fused_computation.162 | convolution fusion | flops 1048576 | bytes 1572992 | tf_op jit(solution)/shard_map/ctq,q->ct/dot_general | solution.py:39
  80.0 1.9 copy.100
  81.9 1.3 copy.75
  83.2 2.2 reshape.113
  85.5 2.8 %fusion.71 = f32[1,512,256]{1,0,2:T(1,128)} fusion(bf16[512,256,4]{0,2,1:T(4,128)(2,1)} %reshape.113, bf16[64]{0:T(256)(128)(2,1)S(1)} %divide_convert_fusion), kind=kOutput, calls=%fused_computation.157 | convolution fusion | flops 1048576 | bytes 1572992 | tf_op jit(solution)/shard_map/ctq,q->ct/dot_general | solution.py:39
  88.3 1.9 copy.95
  90.2 1.3 copy.76
  91.5 2.2 reshape.114
  93.7 2.8 %fusion.72 = f32[1,512,256]{1,0,2:T(1,128)} fusion(bf16[512,256,4]{0,2,1:T(4,128)(2,1)} %reshape.114, bf16[64]{0:T(256)(128)(2,1)S(1)} %divide_convert_fusion), kind=kOutput, calls=%fused_computation.158 | convolution fusion | flops 1048576 | bytes 1572992 | tf_op jit(solution)/shard_map/ctq,q->ct/dot_general | solution.py:39
  96.5 1.9 copy.96
  98.5 1.3 copy.77
  99.8 1.3 reshape.115
  101.1 1.6 fusion.73
  102.7 1.9 copy.97
  109.1 2.9 %fusion.75 = f32[1,512,256]{1,0,2:T(1,128)} fusion(bf16[512,256,4]{0,2,1:T(4,128)(2,1)} %reshape.117, bf16[64]{0:T(256)(128)(2,1)S(1)} %divide_convert_fusion), kind=kOutput, calls=%fused_computation.161 | convolution fusion | flops 1048576 | bytes 1572992 | tf_op jit(solution)/shard_map/ctq,q->ct/dot_general | solution.py:39
  112.0 1.9 copy.99
  114.0 3.6 %fusion.43 = bf16[512,256]{1,0:T(8,128)(2,1)} fusion(f32[1,512,256]{2,1,0:T(8,128)S(1)} %copy-done.5, f32[1,512,256]{2,1,0:T(8,128)} %copy.100, f32[1,512,256]{2,1,0:T(8,128)} %copy.99, f32[1,512,256]{2,1,0:T(8,128)} %copy.98, f32[1,512,256]{2,1,0:T(8,128)} %copy.97, f32[1,512,256]{2,1,0:T(8,128)} %copy.96, f32[1,512,256]{2,1,0:T(8,128)} %copy.95, ...), kind=kLoop, calls=%fused_computation.67 | loop fusion | flops 2097152 | bytes 8650752 | tf_op jit(solution)/shard_map/convert_element_type | solution.py:42
  117.6 7.2 %all-to-all-start = ((bf16[16,32,256]{2,1,0:T(8,128)(2,1)}), bf16[16,32,256]{2,1,0:T(8,128)(2,1)S(1)}, u32[]{:S(2)}, u32[]{:S(2)}) async-start(bf16[16,32,256]{2,1,0:T(8,128)(2,1)} %bitcast.39), calls=%async_computation | async-start | bytes 524288 | tf_op jit(solution)/shard_map/all_to_all | solution.py:106
  124.9 2.5 %cosine_convert_fusion = (bf16[512,192]{1,0:T(8,128)(2,1)S(1)}, bf16[512,192]{1,0:T(8,128)(2,1)S(1)}) fusion(s32[192]{0:T(256)S(1)} %iota_add_fusion.1), kind=kLoop, calls=%fused_computation.83 | loop fusion | flops 1671168 | bytes 393984 | tf_op jit(solution)/shard_map/convert.10
  127.4 7.5 %all-to-all-done = bf16[16,32,256]{2,1,0:T(8,128)(2,1)S(1)} async-done(((bf16[16,32,256]{2,1,0:T(8,128)(2,1)}), bf16[16,32,256]{2,1,0:T(8,128)(2,1)S(1)}, u32[]{:S(2)}, u32[]{:S(2)}) %all-to-all-start) | async-done | bytes 262176 | tf_op jit(solution)/shard_map/all_to_all | solution.py:106
  137.8 1.5 copy.84
  139.3 41.1 %all-gather.2.cloned.1.call-done = bf16[512,8,384]{2,1,0:T(8,128)(2,1)} async-done(((bf16[32,8,384]{2,1,0:T(8,128)(2,1)}), bf16[512,8,384]{2,1,0:T(8,128)(2,1)}) %all-gather.2.cloned.1.call-update) | async-done | bytes 3145744 | tf_op jit(solution)/shard_map/all_gather | solution.py:113
  180.4 4.8 %gather_fusion = bf16[512,8,384]{2,1,0:T(8,128)(2,1)} fusion(bf16[512,8,384]{2,1,0:T(8,128)(2,1)} %all-gather.2.cloned.1.call-done, s32[1024]{0:T(1024)S(1)} %pad_clamp_fusion), kind=kCustom, calls=%fused_computation | custom fusion | bytes 6293504 | tf_op jit(solution)/shard_map/jit(_take)/gather | solution.py:116
  185.3 5.3 %copy.83 = bf16[4,128,8,384]{1,2,3,0:T(8,128)(2,1)} copy(bf16[4,128,8,384]{3,2,1,0:T(8,128)(2,1)} %bitcast.237) | data formatting | bytes 6291456 | tf_op jit(solution)/shard_map/jit(_take)/gather | solution.py:116
  190.6 3.9 %select_select_fusion = bf16[4,128,8,384]{1,2,3,0:T(8,128)(2,1)} fusion(bf16[4,128,8,384]{1,2,3,0:T(8,128)(2,1)} %copy.83, pred[4,128]{1,0:T(4,128)(4,1)S(1)} %get-tuple-element.73, pred[4,128]{1,0:T(4,128)(4,1)S(1)} %get-tuple-element.72), kind=kLoop, calls=%fused_computation.44 | loop fusion | flops 3145728 | bytes 6292480 | tf_op jit(solution)/shard_map/jit(_where)/select_n | solution.py:117
  194.5 40.2 %while.10 = (s32[]{:T(128)}, bf16[4,128,32,256]{3,2,1,0:T(8,128)(2,1)}, bf16[4,128,8,384]{1,2,3,0:T(8,128)(2,1)}, bf16[32,8,384]{0,1,2:T(8,128)(2,1)S(1)}, bf16[384,256]{1,0:T(8,128)(2,1)S(1)}, /*index=5*/s32[]{:T(128)}) while((s32[]{:T(128)}, bf16[4,128,32,256]{3,2,1,0:T(8,128)(2,1)}, bf16[4,128,8,384]{1,2,3,0:T(8,128)(2,1)}, ...), condition=%wide.region_3.4_spmd, body=%wide.region_2.3_spmd.sunk | while | flops 862453760 | bytes 49448044 | solution.py:124
  194.5 1.8 fusion.160
  198.8 3.2 %fusion.167 = bf16[1,128,32,256]{3,1,2,0:T(8,128)(2,1)S(1)} fusion(bf16[128,32,384]{0,1,2:T(8,128)(2,1)S(1)} %pad_maximum_fusion.4, bf16[384,256]{1,0:T(8,128)(2,1)S(1)} %get-tuple-element.123), kind=kOutput, calls=%fused_computation.7.clone.1 | convolution fusion | flops 807403520 | bytes 5439488 | tf_op jit(solution)/shard_map/while/body/eval_jaxpr/dot_general | solution.py:88
  202.0 2.5 %copy_dynamic-update-slice_fusion.2 = bf16[4,128,32,256]{3,2,1,0:T(8,128)(2,1)} fusion(bf16[4,128,32,256]{3,2,1,0:T(8,128)(2,1)} %get-tuple-element.114, s32[]{:T(128)} %get-tuple-element.113, bf16[1,128,32,256]{3,1,2,0:T(8,128)(2,1)S(1)} %fusion.167), kind=kLoop, calls=%fused_computation.8.clone.1 | loop fusion | bytes 4194816 | tf_op jit(solution)/shard_map/while/body/jit(dynamic_update_index_in_dim)/dynamic_update_slice | solution.py:124
  204.6 1.8 fusion.160
  208.8 3.2 %fusion.167 = bf16[1,128,32,256]{3,1,2,0:T(8,128)(2,1)S(1)} fusion(bf16[128,32,384]{0,1,2:T(8,128)(2,1)S(1)} %pad_maximum_fusion.4, bf16[384,256]{1,0:T(8,128)(2,1)S(1)} %get-tuple-element.123), kind=kOutput, calls=%fused_computation.7.clone.1 | convolution fusion | flops 807403520 | bytes 5439488 | tf_op jit(solution)/shard_map/while/body/eval_jaxpr/dot_general | solution.py:88
  212.1 2.5 %copy_dynamic-update-slice_fusion.2 = bf16[4,128,32,256]{3,2,1,0:T(8,128)(2,1)} fusion(bf16[4,128,32,256]{3,2,1,0:T(8,128)(2,1)} %get-tuple-element.114, s32[]{:T(128)} %get-tuple-element.113, bf16[1,128,32,256]{3,1,2,0:T(8,128)(2,1)S(1)} %fusion.167), kind=kLoop, calls=%fused_computation.8.clone.1 | loop fusion | bytes 4194816 | tf_op jit(solution)/shard_map/while/body/jit(dynamic_update_index_in_dim)/dynamic_update_slice | solution.py:124
  214.7 1.8 fusion.160
  218.9 3.2 %fusion.167 = bf16[1,128,32,256]{3,1,2,0:T(8,128)(2,1)S(1)} fusion(bf16[128,32,384]{0,1,2:T(8,128)(2,1)S(1)} %pad_maximum_fusion.4, bf16[384,256]{1,0:T(8,128)(2,1)S(1)} %get-tuple-element.123), kind=kOutput, calls=%fused_computation.7.clone.1 | convolution fusion | flops 807403520 | bytes 5439488 | tf_op jit(solution)/shard_map/while/body/eval_jaxpr/dot_general | solution.py:88
  222.2 2.5 %copy_dynamic-update-slice_fusion.2 = bf16[4,128,32,256]{3,2,1,0:T(8,128)(2,1)} fusion(bf16[4,128,32,256]{3,2,1,0:T(8,128)(2,1)} %get-tuple-element.114, s32[]{:T(128)} %get-tuple-element.113, bf16[1,128,32,256]{3,1,2,0:T(8,128)(2,1)S(1)} %fusion.167), kind=kLoop, calls=%fused_computation.8.clone.1 | loop fusion | bytes 4194816 | tf_op jit(solution)/shard_map/while/body/jit(dynamic_update_index_in_dim)/dynamic_update_slice | solution.py:124
  224.7 1.8 fusion.160
  229.0 3.2 %fusion.167 = bf16[1,128,32,256]{3,1,2,0:T(8,128)(2,1)S(1)} fusion(bf16[128,32,384]{0,1,2:T(8,128)(2,1)S(1)} %pad_maximum_fusion.4, bf16[384,256]{1,0:T(8,128)(2,1)S(1)} %get-tuple-element.123), kind=kOutput, calls=%fused_computation.7.clone.1 | convolution fusion | flops 807403520 | bytes 5439488 | tf_op jit(solution)/shard_map/while/body/eval_jaxpr/dot_general | solution.py:88
  232.2 2.5 %copy_dynamic-update-slice_fusion.2 = bf16[4,128,32,256]{3,2,1,0:T(8,128)(2,1)} fusion(bf16[4,128,32,256]{3,2,1,0:T(8,128)(2,1)} %get-tuple-element.114, s32[]{:T(128)} %get-tuple-element.113, bf16[1,128,32,256]{3,1,2,0:T(8,128)(2,1)S(1)} %fusion.167), kind=kLoop, calls=%fused_computation.8.clone.1 | loop fusion | bytes 4194816 | tf_op jit(solution)/shard_map/while/body/jit(dynamic_update_index_in_dim)/dynamic_update_slice | solution.py:124
  (113 shorter events, 38.2 us)
Async XLA Ops:
  7.5 7.6 %collective-permute-start = (bf16[512,60]{1,0:T(8,128)(2,1)S(1)}, bf16[512,60]{1,0:T(8,128)(2,1)S(1)}, u32[]{:S(2)}, u32[]{:S(2)}) collective-permute-start(bf16[512,60]{1,0:T(8,128)(2,1)S(1)} %slice.114), channel_id=1, source_target_pairs={{0,1},{1,2},{2,3},{3,4},{4,5},{5,6},{6,7},{7,8},{8,9},{9,10},{10,1... | collective-permute-start | bytes 184328 | tf_op jit(solution)/shard_map/ppermute | solution.py:20
  12.2 2.9 %copy-start = (bf16[512,1024]{1,0:T(8,128)(2,1)S(1)}, bf16[512,1024]{1,0:T(8,128)(2,1)}, u32[]{:S(2)}) copy-start(bf16[512,1024]{1,0:T(8,128)(2,1)} %param.5) | copy-start | bytes 3145732
  75.0 6.9 %copy-start.3 = (bf16[512,1024]{1,0:T(8,128)(2,1)S(1)}, bf16[512,1024]{1,0:T(8,128)(2,1)}, u32[]{:S(2)}) copy-start(bf16[512,1024]{1,0:T(8,128)(2,1)} %get-tuple-element.62) | copy-start | bytes 3145732
  83.2 6.9 %copy-start.2 = (bf16[512,1024]{1,0:T(8,128)(2,1)S(1)}, bf16[512,1024]{1,0:T(8,128)(2,1)}, u32[]{:S(2)}) copy-start(bf16[512,1024]{1,0:T(8,128)(2,1)} %get-tuple-element.63) | copy-start | bytes 3145732
  91.5 7.0 %copy-start.1 = (bf16[512,1024]{1,0:T(8,128)(2,1)S(1)}, bf16[512,1024]{1,0:T(8,128)(2,1)}, u32[]{:S(2)}) copy-start(bf16[512,1024]{1,0:T(8,128)(2,1)} %get-tuple-element.64) | copy-start | bytes 3145732
  107.9 6.0 %copy-start.5 = (f32[1,512,256]{2,1,0:T(8,128)S(1)}, f32[1,512,256]{2,1,0:T(8,128)}, u32[]{:S(2)}) copy-start(f32[1,512,256]{2,1,0:T(8,128)} %copy.101) | copy-start | bytes 1572868
  107.9 6.0 %copy-start.6 = (f32[1,512,256]{2,1,0:T(8,128)S(1)}, f32[1,512,256]{2,1,0:T(8,128)}, u32[]{:S(2)}) copy-start(f32[1,512,256]{2,1,0:T(8,128)} %copy.86) | copy-start | bytes 1572868
  107.9 6.0 %copy-start.7 = (f32[1,512,256]{2,1,0:T(8,128)S(1)}, f32[1,512,256]{2,1,0:T(8,128)}, u32[]{:S(2)}) copy-start(f32[1,512,256]{2,1,0:T(8,128)} %copy.87) | copy-start | bytes 1572868
  107.9 6.0 %copy-start.8 = (f32[1,512,256]{2,1,0:T(8,128)S(1)}, f32[1,512,256]{2,1,0:T(8,128)}, u32[]{:S(2)}) copy-start(f32[1,512,256]{2,1,0:T(8,128)} %copy.88) | copy-start | bytes 1572868
  109.1 4.9 %copy-start.9 = (f32[1,512,256]{2,1,0:T(8,128)S(1)}, f32[1,512,256]{2,1,0:T(8,128)}, u32[]{:S(2)}) copy-start(f32[1,512,256]{2,1,0:T(8,128)} %copy.89) | copy-start | bytes 1572868
  109.1 4.9 %copy-start.10 = (f32[1,512,256]{2,1,0:T(8,128)S(1)}, f32[1,512,256]{2,1,0:T(8,128)}, u32[]{:S(2)}) copy-start(f32[1,512,256]{2,1,0:T(8,128)} %copy.90) | copy-start | bytes 1572868
  113.9 10.9 %copy-start.12 = (s32[32]{0:T(128)S(1)}, s32[32]{0:T(128)}, u32[]{:S(2)}) copy-start(s32[32]{0:T(128)} %param.7) | copy-start | bytes 388
  117.6 17.3 %all-to-all-start = ((bf16[16,32,256]{2,1,0:T(8,128)(2,1)}), bf16[16,32,256]{2,1,0:T(8,128)(2,1)S(1)}, u32[]{:S(2)}, u32[]{:S(2)}) async-start(bf16[16,32,256]{2,1,0:T(8,128)(2,1)} %bitcast.39), calls=%async_computation | async-start | bytes 524288 | tf_op jit(solution)/shard_map/all_to_all | solution.py:106
  124.8 55.6 %all-gather.2.cloned.1.call-start = ((), (), s32[]{:S(2)}) async-start(), calls=%async_computation.1 | async-start | bytes 3342336 | tf_op jit(solution)/shard_map/all_gather | solution.py:113
  134.9 1.9 copy-start.11
  194.5 2.0 copy-start.4
  204.6 2.0 copy-start.4
  214.6 2.0 copy-start.4
  224.7 2.0 copy-start.4
Sparse Core Ops, SparseCore 0:
  136.9 43.4 all-gather.1
where the time goes:
time: 243 us; the launch traced here: 242 us
  local copies, waits for them, and re-layouts  87.2 us (36%)
  matrix products  58.7 us (24%)
  waiting for transfers between devices  48.6 us (20%)
  other arithmetic  23.2 us (10%)
  between operations  13.8 us (6%)
  starting transfers between devices  9.62 us (4%)
    all_gather x1, waiting for transfers between devices, body(): shard_rows = lax.all_gather(whitened, 'chan', axis=0, tiled=True)  41.1 us
    dot_general x16, matrix products, decimate(): jnp.einsum('ctq,q->ct', window_rows, weights, preferred_element_type=jnp....  30.8 us
    dot_general x16, local copies, waits for them, and re-layouts, decimate(): jnp.einsum('ctq,q->ct', window_rows, weights, preferred_element_type=jnp....  22.7 us
    slice x15, local copies, waits for them, and re-layouts, decimate(): padded[:, 4 * stride:4 * stride + 4 * out_length]  19.8 us
    reshape x16, local copies, waits for them, and re-layouts, decimate(): padded[:, 4 * stride:4 * stride + 4 * out_length]  18.9 us
    dot_general x4, matrix products, correlate(): jnp.dot(cross.reshape(source_count * recv_count, 2 * NF), delays, preferr...  13 us
    gather x2, local copies, waits for them, and re-layouts, body(): jnp.take(shard_rows, jnp.clip(source_index, 0, row_count - 1), axis=0)  10.2 us
    dynamic_update_slice x4, local copies, waits for them, and re-layouts, body(): result = lax.map(one_block, blocks)  10.1 us
  transfers between devices with their start and end apart: 3, of which 2 were waited for; matrix products, arithmetic and copies ran while one was open for 4% of the time, Pallas kernels for 0%

commit v1 on v0

--- a/solution.py
+++ b/solution.py
@@ -1,8 +1,13 @@
+import functools
 import math
 
 import jax
 import jax.numpy as jnp
+import ml_dtypes
+import numpy as np
 from jax import lax
+from jax.experimental import pallas as pl
+from jax.experimental.pallas import tpu as pltpu
 from jax.sharding import PartitionSpec as P
 
 SEGS = 8
@@ -125,8 +130,342 @@
     return result.reshape(SOURCES, per_device, LAGS)
 
 
+CHIPS = SEGS
+TAIL = 128
+GROUP = 16
+GROUPS = NF // GROUP
+FLAG_ROWS = 16
+ROWS = 2 * NF + FLAG_ROWS
+CHUNKS = ((0, 112), (112, 96), (208, 96), (304, 96))
+MIB = 1024 * 1024
+
+
+def numpy_taps():
+    k = np.arange(TAPS, dtype=np.float64)
+    window = 0.5 - 0.5 * np.cos(2.0 * np.pi * (k + 0.5) / TAPS)
+    taps = 0.2 * np.sinc(0.2 * (k - (TAPS - 1) / 2.0)) * window
+    return (taps / taps.sum()).astype(ml_dtypes.bfloat16)
+
+
+def decimation_tables(raw_count):
+    taps = numpy_taps()
+    n = np.arange(raw_count // 4)[None, :]
+
+    def table(position):
+        k = 4 * n + 3 - position[:, None]
+        return np.where((k >= 0) & (k < TAPS), taps[np.clip(k, 0, TAPS - 1)], 0).astype(ml_dtypes.bfloat16)
+
+    return table(np.arange(raw_count)), table(np.arange(-TAIL, 0))
+
+
+def numpy_fourier():
+    frequency = FBASE + np.arange(NF)[:, None]
+    angles = 2.0 * np.pi * (frequency * np.arange(NSEG)[None, :] % NSEG) / NSEG
+    return np.concatenate([np.cos(angles), -np.sin(angles)], axis=0).astype(ml_dtypes.bfloat16)
+
+
+def numpy_delays():
+    frequency = FBASE + np.arange(NF)[:, None]
+    delays = np.arange(LAGS)[None, :] - LAGS // 2
+    angles = 2.0 * np.pi * (frequency * delays % NSEG) / NSEG
+    pair = np.stack([np.cos(angles), -np.sin(angles)]).reshape(2, GROUPS, GROUP, LAGS)
+    return pair.transpose(1, 0, 2, 3).reshape(2 * NF, LAGS).astype(ml_dtypes.bfloat16)
+
+
+def table_rows(raw_count):
+    ends = np.cumsum([0, raw_count, TAIL, 2 * NF, 2 * NF, 2 * NF])
+    return [slice(int(a), int(b)) for a, b in zip(ends[:-1], ends[1:])]
+
+
+def chip_at(place):
+    upper = place // (CHIPS // 2)
+    return (1 - upper) * 2 * place + upper * (2 * CHIPS - 1 - 2 * place)
+
+
+def spectra_kernel(
+    x_ref, flags_ref, table_ref, g_ref, xs, halo,
+    own_sem, pair_send, pair_recv, halo_send, halo_recv, ring_send, ring_recv, side_send, side_recv,
+):
+    me = lax.axis_index("chan")
+    core = lax.rem(me, 2)
+    chip = me // 2
+    z = chip // 2
+    y = lax.rem(chip, 2)
+    place = z + y * (CHIPS - 1 - 2 * z)
+    forward = chip_at(lax.rem(place + 1, CHIPS)) * 2 + core
+    backward = chip_at(lax.rem(place + CHIPS - 1, CHIPS)) * 2 + core
+    sibling = chip * 2 + 1 - core
+    half = x_ref.shape[0] // 2
+    raw_count = x_ref.shape[1]
+    gives_halo = jnp.logical_and(core == 1, chip < CHIPS - 1)
+    takes_halo = chip > 0
+
+    own = pltpu.make_async_copy(x_ref.at[pl.ds(core * half, half), :], xs.at[core], own_sem)
+    own.start()
+    barrier = pltpu.get_barrier_semaphore()
+
+    def greet(device):
+        pl.semaphore_signal(barrier, inc=1, device_id={"chan": device}, device_id_type=pl.DeviceIdType.MESH)
+
+    for device in (sibling, forward, backward):
+        greet(device)
+
+    @pl.when(takes_halo)
+    def _():
+        greet(me - core - 1)
+
+    @pl.when(gives_halo)
+    def _():
+        greet(me + 1)
+        greet(me + 2)
+
+    pl.semaphore_wait(barrier, 3 + jnp.where(takes_halo, 1, 0) + jnp.where(gives_halo, 2, 0))
+
+    def send(source, target, send_sem, recv_sem, device):
+        return pltpu.make_async_remote_copy(
+            src_ref=source, dst_ref=target, send_sem=send_sem, recv_sem=recv_sem,
+            device_id={"chan": device}, device_id_type=pl.DeviceIdType.MESH,
+        )
+
+    def halo_copy(h):
+        return send(
+            x_ref.at[pl.ds(h * half, half), pl.ds(raw_count - TAIL, TAIL)], halo,
+            halo_send.at[h], halo_recv, me + 1 + h,
+        )
+
+    @pl.when(gives_halo)
+    def _():
+        halo_copy(0).start()
+        halo_copy(1).start()
+
+    pair = send(
+        x_ref.at[pl.ds((1 - core) * half, half), :], xs.at[core], pair_send, pair_recv, sibling
+    )
+    pair.start()
+
+    @pl.when(chip == 0)
+    def _():
+        halo[...] = jnp.zeros_like(halo)
+
+    @pl.when(takes_halo)
+    def _():
+        halo_copy(0).wait_recv()
+
+    own.wait()
+    pair_in = send(x_ref.at[pl.ds(0, half), :], xs.at[1 - core], pair_send, pair_recv, sibling)
+    pair_in.wait_recv()
+
+    def product(a, b):
+        return jnp.dot(a, b, preferred_element_type=jnp.float32)
+
+    block, tail, before, after, _ = table_rows(raw_count)
+    first = product(xs[0], table_ref[block]) + product(halo[...], table_ref[tail])
+    second = product(xs[1], table_ref[block]) + product(xs[0, :, raw_count - TAIL :], table_ref[tail])
+
+    def transform(table, decimated):
+        return lax.dot_general(
+            table, decimated.astype(jnp.bfloat16), (((1,), (1,)), ((), ())), preferred_element_type=jnp.float32
+        )
+
+    spectrum = transform(table_ref[before], first) + transform(table_ref[after], second)
+    real_part = spectrum[:NF]
+    imag_part = spectrum[NF:]
+    power = real_part * real_part + imag_part * imag_part
+    average = jnp.mean(power, axis=0, keepdims=True)
+    factor = lax.rsqrt(power + 0.1 * average + 1e-05)
+    g_ref[me, 0:NF, :] = (real_part * factor).astype(jnp.bfloat16)
+    g_ref[me, NF : 2 * NF, :] = (imag_part * factor).astype(jnp.bfloat16)
+    g_ref[me, 2 * NF : ROWS, :] = flags_ref[...]
+
+    def piece(distance, c, side):
+        device = chip_at(lax.rem(place + CHIPS - distance, CHIPS)) * 2 + side
+        return g_ref.at[device, pl.ds(CHUNKS[c][0], CHUNKS[c][1]), :]
+
+    def onward(way, step, c):
+        view = piece(step if way == 0 else (CHIPS - step) % CHIPS, c, core)
+        return send(
+            view, view, ring_send.at[way, step, c], ring_recv.at[way, step, c], backward if way else forward
+        )
+
+    def across(distance, c, side):
+        view = piece(distance, c, side)
+        return send(view, view, side_send.at[distance, c], side_recv.at[distance, c], sibling)
+
+    last = CHIPS // 2 - 1
+    count = len(CHUNKS)
+    moves = [
+        [(way, c) for c in range(count) for way in range(2) if step < last or way == c // (count // 2)]
+        for step in range(last + 1)
+    ]
+    for way, c in moves[0]:
+        onward(way, 0, c).start()
+    for c in range(count):
+        across(0, c, core).start()
+    for step in range(last + 1):
+        for way, c in moves[step]:
+            distance = step + 1 if way == 0 else CHIPS - step - 1
+            view = piece(distance, c, core)
+            send(view, view, ring_send.at[way, step, c], ring_recv.at[way, step, c], forward).wait_recv()
+            if step < last and (way, c) in moves[step + 1]:
+                onward(way, step + 1, c).start()
+            across(distance, c, core).start()
+    for step in range(last + 1):
+        for way, c in moves[step]:
+            onward(way, step, c).wait_send()
+    for distance in range(CHIPS):
+        for c in range(count):
+            across(distance, c, core).wait_send()
+            across(distance, c, 1 - core).wait_recv()
+    pair.wait_send()
+
+    @pl.when(gives_halo)
+    def _():
+        halo_copy(0).wait_send()
+        halo_copy(1).wait_send()
+
+
+def correlate_kernel(
+    delays, me_ref, index_ref, g_ref, table_ref, out_ref, weights, cross, mixed, result, out_sem
+):
+    half = g_ref.shape[2]
+    blocks, sources, receivers, _ = result.shape
+    side = mixed.shape[2] // sources
+    flags = g_ref[0, 2 * NF : ROWS, :].astype(jnp.float32)
+    for device in range(1, 2 * CHIPS):
+        flags = flags + g_ref[device, 2 * NF : ROWS, :].astype(jnp.float32)
+    flags = [flags[h : h + 1, :].astype(jnp.bfloat16) for h in range(2)]
+
+    def spectra(group, h):
+        parts = [
+            g_ref[2 * w + h, c * NF + group * GROUP : c * NF + (group + 1) * GROUP, :]
+            for c in range(2)
+            for w in range(SEGS)
+        ]
+        return jnp.concatenate(parts, axis=0) * flags[h]
+
+    def chooser(h, wanted, shape, axis):
+        channel = lax.broadcasted_iota(jnp.int32, shape, axis) + h * half
+        return jnp.where(channel == wanted, 1.0, 0.0).astype(jnp.bfloat16)
+
+    mine = lax.broadcasted_iota(jnp.int32, (receivers, half), 0) + me_ref[0] * receivers
+    pick = [chooser(h, mine, (receivers, half), 1) for h in range(2)]
+    width = 2 * SEGS * GROUP
+    lane = lax.broadcasted_iota(jnp.int32, (GROUP, width), 1)
+    same = lax.rem(lane, GROUP) == lax.broadcasted_iota(jnp.int32, (GROUP, width), 0)
+    same = jnp.where(same, 1.0, 0.0)[None]
+    for group in range(GROUPS):
+        rows = jnp.zeros((receivers, width), jnp.float32)
+        for h in range(2):
+            rows = rows + lax.dot_general(
+                pick[h], spectra(group, h), (((1,), (1,)), ((), ())), preferred_element_type=jnp.float32
+            )
+        turned = jnp.concatenate([-rows[:, width // 2 :], rows[:, : width // 2]], axis=1)
+        weights[group, :, 0:GROUP, :] = (rows[:, None, :] * same).astype(jnp.bfloat16)
+        weights[group, :, GROUP : 2 * GROUP, :] = (turned[:, None, :] * same).astype(jnp.bfloat16)
+
+    def write(at, part):
+        return pltpu.make_async_copy(
+            result.at[at, :, pl.ds(part * side, side), :],
+            out_ref.at[pl.ds(at * sources, sources), pl.ds(part * side, side), :],
+            out_sem.at[at, part],
+        )
+
+    def one_block(at, carry):
+        wanted = index_ref[:, pl.ds(pl.multiple_of(at * sources, sources), sources)]
+        chosen_by = [chooser(h, wanted, (half, sources), 0) for h in range(2)]
+        part = 8
+        for group in range(GROUPS):
+            chosen = jnp.zeros((width, sources), jnp.float32)
+            for h in range(2):
+                chosen = chosen + jnp.dot(spectra(group, h), chosen_by[h], preferred_element_type=jnp.float32)
+            chosen = chosen.astype(jnp.bfloat16)
+            for r in range(0, receivers, part):
+                block = weights[group, r : r + part].reshape(part * 2 * GROUP, width)
+                product = jnp.dot(block, chosen, preferred_element_type=jnp.float32)
+                cross[r : r + part, group * 2 * GROUP : (group + 1) * 2 * GROUP, :] = product.astype(
+                    jnp.bfloat16
+                ).reshape(part, 2 * GROUP, sources)
+        for r in range(receivers):
+            lagged = lax.dot_general(
+                cross[r], table_ref[delays], (((0,), (0,)), ((), ())), preferred_element_type=jnp.float32
+            )
+            slot = r // side % 2
+            for l in range(0, LAGS, 128):
+                mixed[slot, l // 128, pl.ds(r % side, sources, stride=side), :] = lagged[:, l : l + 128] * (
+                    1.0 / math.sqrt(SEGS * NF)
+                )
+            if r % side == side - 1:
+                for l in range(0, LAGS, 128):
+                    done = mixed[slot, l // 128].reshape(sources, side, 128).astype(jnp.bfloat16)
+                    result[at, :, r - side + 1 : r + 1, l : l + 128] = done
+                write(at, r // side).start()
+        return carry
+
+    lax.fori_loop(0, blocks, one_block, 0)
+    for at in range(blocks):
+        for part in range(receivers // side):
+            write(at, part).wait()
+
+
+def fast_body(recording, source_index, channel_mask):
+    channels, raw_count = recording.shape
+    half = channels // 2
+    per_device = channel_mask.shape[0]
+    me = lax.axis_index("chan")
+    spread = jnp.tile(channel_mask, channels // per_device)
+    mine = jnp.arange(channels, dtype=jnp.int32) // per_device == me
+    flags = jnp.where(mine, spread, 0).astype(jnp.bfloat16).reshape(2, half)
+    flags = jnp.pad(flags, ((0, FLAG_ROWS - 2), (0, 0)))
+    block_table, tail_table = decimation_tables(raw_count)
+    fourier = numpy_fourier()
+    tables = [block_table, tail_table, fourier[:, : NSEG // 2], fourier[:, NSEG // 2 :], numpy_delays()]
+    tables = jnp.asarray(np.concatenate(tables))
+    vmem = pl.BlockSpec(memory_space=pltpu.VMEM)
+    hbm = pl.BlockSpec(memory_space=pltpu.HBM)
+    dma = pltpu.SemaphoreType.DMA
+    bf16 = jnp.bfloat16
+    count = len(CHUNKS)
+    gathered = pl.pallas_call(
+        spectra_kernel,
+        out_shape=jax.ShapeDtypeStruct((2 * CHIPS, ROWS, half), jnp.bfloat16),
+        in_specs=[hbm, vmem, vmem],
+        out_specs=vmem,
+        scratch_shapes=[
+            pltpu.VMEM((2, half, raw_count), jnp.bfloat16),
+            pltpu.VMEM((half, TAIL), jnp.bfloat16),
+            dma, dma, dma, dma((2,)), dma,
+            dma((2, CHIPS // 2, count)), dma((2, CHIPS // 2, count)), dma((CHIPS, count)), dma((CHIPS, count)),
+        ],
+        compiler_params=pltpu.CompilerParams(
+            collective_id=0, has_side_effects=True, vmem_limit_bytes=24 * MIB
+        ),
+        name="spectra",
+    )(recording, flags, tables)
+    sources = source_index.shape[0]
+    block = 256
+    receivers = per_device
+    blocks = sources // block
+    side = 16
+    return pl.pallas_call(
+        functools.partial(correlate_kernel, table_rows(raw_count)[-1]),
+        out_shape=jax.ShapeDtypeStruct((sources, receivers, LAGS), bf16),
+        in_specs=[pl.BlockSpec(memory_space=pltpu.SMEM), vmem, vmem, vmem],
+        out_specs=hbm,
+        scratch_shapes=[
+            pltpu.VMEM((GROUPS, receivers, 2 * GROUP, 2 * SEGS * GROUP), bf16),
+            pltpu.VMEM((receivers, 2 * NF, block), bf16),
+            pltpu.VMEM((2, LAGS // 128, block * side, 128), jnp.float32),
+            pltpu.VMEM((blocks, block, receivers, LAGS), bf16),
+            dma((blocks, receivers // side)),
+        ],
+        compiler_params=pltpu.CompilerParams(vmem_limit_bytes=44 * MIB),
+        name="correlate",
+    )(me.reshape(1), source_index.reshape(1, sources), gathered, tables)
+
+
 def solution(mesh):
     placed = (P("fiber", "chan"), P("fiber"), P(("fiber", "chan")))
+    chosen_body = fast_body if mesh.shape["chan"] == 2 * SEGS else body
     return jax.shard_map(
-        body, mesh=mesh, in_specs=placed, out_specs=P("fiber", "chan", None), check_vma=False
-    )
+        chosen_body, mesh=mesh, in_specs=placed, out_specs=P("fiber", "chan", None), check_vma=False
+    )

time: 243 us -> 56.6 us (0.23)
  local copies, waits for them, and re-layouts: 87.2 us -> 3.26 us
  matrix products: 58.7 us -> 0 us
  Pallas kernels: 0 us -> 53.1 us
  waiting for transfers between devices: 48.6 us -> 0 us
  other arithmetic: 23.2 us -> 0.02 us
  between operations: 13.8 us -> 0.04 us
  starting transfers between devices: 9.62 us -> 0 us
    dot_general x37 -> x0, matrix products: 58.7 us -> none  [the longest x16 30.8 us: decimate(): jnp.einsum('ctq,q->ct', window_rows, weights, preferred_element_type=jnp....]
    pallas_call x0 -> x2, Pallas kernels: none -> 53.1 us  [the longest x1 28.9 us: fast_body(): pl.pallas_call(spectra_kernel, out_shape=jax.ShapeDtypeStruct((2 * CHIPS,...]
    all_gather x1 -> x0, waiting for transfers between devices: 41.1 us -> none  [body(): shard_rows = lax.all_gather(whitened, 'chan', axis=0, tiled=True)]
    dot_general x32 -> x0, local copies, waits for them, and re-layouts: 23.2 us -> none  [the longest x16 22.7 us: decimate(): jnp.einsum('ctq,q->ct', window_rows, weights, preferred_element_type=jnp....]
    slice x16 -> x0, local copies, waits for them, and re-layouts: 20.8 us -> none  [the longest x15 19.8 us: decimate(): padded[:, 4 * stride:4 * stride + 4 * out_length]]
    reshape x17 -> x0, local copies, waits for them, and re-layouts: 19 us -> none  [the longest x16 18.9 us: decimate(): padded[:, 4 * stride:4 * stride + 4 * out_length]]
    gather x2 -> x0, local copies, waits for them, and re-layouts: 10.2 us -> none  [body(): jnp.take(shard_rows, jnp.clip(source_index, 0, row_count - 1), axis=0)]
    dynamic_update_slice x4 -> x0, local copies, waits for them, and re-layouts: 10.1 us -> none  [body(): result = lax.map(one_block, blocks)]
  transfers between devices with their start and end apart: 3 -> 0, of which waited for: 2 -> 0; matrix products, arithmetic and copies ran while one was open for 4% -> 0% of each run, Pallas kernels for 0% -> 0%
where the time goes in v1:
time: 56.6 us; the launch traced here: 56.4 us
  Pallas kernels  53.1 us (94%)
  local copies, waits for them, and re-layouts  3.26 us (6%)
    pallas_call x1, Pallas kernels, fast_body(): pl.pallas_call(spectra_kernel, out_shape=jax.ShapeDtypeStruct((2 * CHIPS,...  28.9 us
    pallas_call x1, Pallas kernels, fast_body(): pl.pallas_call(functools.partial(correlate_kernel, table_rows(raw_count)[...  24.1 us
    unnamed x8, local copies, waits for them, and re-layouts  2.5 us

profile of v1, /device:TPU:0, one launch (start us, length us, event | category | flops | bytes accessed | tf_op | source)
XLA Modules:
  0.0 56.4 jit_solution(11575427698454553782)
XLA Ops:
  0.0 0.0 copy-start.3
  0.0 0.7 %tile.11 = s32[8,32]{1,0:T(8,128)S(1)} broadcast(s32[32]{0:T(128)} %param.6), dimensions={1} | broadcast | bytes 1152 | tf_op jit(solution)/shard_map/tile | solution.py:415
  0.7 0.1 tile.12
  0.8 0.0 copy-start
  0.8 1.3 %copy-done = bf16[2304,256]{1,0:T(8,128)(2,1)S(1)} copy-done((bf16[2304,256]{1,0:T(8,128)(2,1)S(1)}, bf16[2304,256]{1,0:T(8,128)(2,1)}, u32[]{:S(2)}) %copy-start) | copy-done | bytes 1179672
  2.1 0.0 copy-start.2
  2.1 1.2 %copy-done.2 = bf16[512,1024]{1,0:T(8,128)(2,1)S(1)} copy-done((bf16[512,1024]{1,0:T(8,128)(2,1)S(1)}, bf16[512,1024]{1,0:T(8,128)(2,1)}, u32[]{:S(2)}) %copy-start.2) | copy-done | bytes 1048600
  3.3 0.0 copy-start.1
  3.3 28.9 %spectra.1.g_ref = bf16[16,400,256]{2,1,0:T(8,128)(2,1)S(1)} custom-call(bf16[512,1024]{1,0:T(8,128)(2,1)S(1)} %copy-done.2, bf16[16,256]{1,0:T(8,128)(2,1)S(1)} %pad.4.flags_ref, bf16[2304,256]{1,0:T(8,128)(2,1)S(1)} %copy-done), custom_call_target="tpu_custom_call" | custom-call | tf_op jit(solution)/shard_map/spectra/pallas_call | solution.py:428
  32.2 0.0 copy-done.3
  32.2 0.0 copy-done.1
  32.2 24.1 %correlate.1 = bf16[512,32,256]{2,1,0:T(8,128)(2,1)} custom-call(s32[1]{0:T(128)} %bitcast.me_ref, s32[1,512]{1,0:T(1,128)S(1)} %bitcast.2, bf16[16,400,256]{2,1,0:T(8,128)(2,1)S(1)} %spectra.1.g_ref, bf16[2304,256]{1,0:T(8,128)(2,1)S(1)} %copy-done.1), custom_call_target="tpu_custom_call" | custom-call | tf_op jit(solution)/shard_map/correlate/pallas_call | solution.py:449
  (2 shorter events, 0.0 us)
Async XLA Ops:
  0.0 32.2 %copy-start.3 = (s32[512]{0:T(512)S(1)}, s32[512]{0:T(512)}, u32[]{:S(2)}) copy-start(s32[512]{0:T(512)} %param.5) | copy-start | bytes 6148
  0.8 1.3 %copy-start = (bf16[2304,256]{1,0:T(8,128)(2,1)S(1)}, bf16[2304,256]{1,0:T(8,128)(2,1)}, u32[]{:S(2)}) copy-start(bf16[2304,256]{1,0:T(8,128)(2,1)} %constant.33.clone.table_ref) | copy-start | bytes 3538948
  2.1 1.2 %copy-start.2 = (bf16[512,1024]{1,0:T(8,128)(2,1)S(1)}, bf16[512,1024]{1,0:T(8,128)(2,1)}, u32[]{:S(2)}) copy-start(bf16[512,1024]{1,0:T(8,128)(2,1)} %x_ref.1) | copy-start | bytes 3145732
  3.3 28.9 %copy-start.1 = (bf16[2304,256]{1,0:T(8,128)(2,1)S(1)}, bf16[2304,256]{1,0:T(8,128)(2,1)}, u32[]{:S(2)}) copy-start(bf16[2304,256]{1,0:T(8,128)(2,1)} %constant.33.clone.table_ref) | copy-start | bytes 3538948

commit v2 on v1

--- a/solution.py
+++ b/solution.py
@@ -1,4 +1,3 @@
-import functools
 import math
 
 import jax
@@ -135,6 +134,7 @@
 GROUP = 16
 GROUPS = NF // GROUP
 FLAG_ROWS = 16
+QUAD = 4
 ROWS = 2 * NF + FLAG_ROWS
 CHUNKS = ((0, 112), (112, 96), (208, 96), (304, 96))
 MIB = 1024 * 1024
@@ -168,12 +168,14 @@
     frequency = FBASE + np.arange(NF)[:, None]
     delays = np.arange(LAGS)[None, :] - LAGS // 2
     angles = 2.0 * np.pi * (frequency * delays % NSEG) / NSEG
-    pair = np.stack([np.cos(angles), -np.sin(angles)]).reshape(2, GROUPS, GROUP, LAGS)
-    return pair.transpose(1, 0, 2, 3).reshape(2 * NF, LAGS).astype(ml_dtypes.bfloat16)
+    pair = np.stack([np.cos(angles), -np.sin(angles)]).reshape(2, GROUPS, GROUP, LAGS).transpose(1, 0, 2, 3)
+    slot = np.arange(GROUPS)
+    order = [slot // QUAD * QUAD + (slot - a) % QUAD for a in range(QUAD)]
+    return np.concatenate([pair[at].reshape(2 * NF, LAGS) for at in order]).astype(ml_dtypes.bfloat16)
 
 
 def table_rows(raw_count):
-    ends = np.cumsum([0, raw_count, TAIL, 2 * NF, 2 * NF, 2 * NF])
+    ends = np.cumsum([0, raw_count, TAIL, 2 * NF, 2 * NF])
     return [slice(int(a), int(b)) for a, b in zip(ends[:-1], ends[1:])]
 
 
@@ -258,7 +260,7 @@
     def product(a, b):
         return jnp.dot(a, b, preferred_element_type=jnp.float32)
 
-    block, tail, before, after, _ = table_rows(raw_count)
+    block, tail, before, after = table_rows(raw_count)
     first = product(xs[0], table_ref[block]) + product(halo[...], table_ref[tail])
     second = product(xs[1], table_ref[block]) + product(xs[0, :, raw_count - TAIL :], table_ref[tail])
 
@@ -275,7 +277,15 @@
     factor = lax.rsqrt(power + 0.1 * average + 1e-05)
     g_ref[me, 0:NF, :] = (real_part * factor).astype(jnp.bfloat16)
     g_ref[me, NF : 2 * NF, :] = (imag_part * factor).astype(jnp.bfloat16)
-    g_ref[me, 2 * NF : ROWS, :] = flags_ref[...]
+    per_device = flags_ref.shape[1]
+    to_row = me * per_device // half
+    to_lane = me * per_device - to_row * half
+    lane = lax.broadcasted_iota(jnp.int32, (per_device, half), 1)
+    spot = lane == lax.broadcasted_iota(jnp.int32, (per_device, half), 0) + to_lane
+    row = lax.broadcasted_iota(jnp.int32, (FLAG_ROWS, per_device), 0)
+    held = jnp.where(row == to_row, flags_ref[...], 0).astype(jnp.float32).astype(jnp.bfloat16)
+    placed = product(held, jnp.where(spot, 1.0, 0.0).astype(jnp.bfloat16))
+    g_ref[me, 2 * NF : ROWS, :] = placed.astype(jnp.bfloat16)
 
     def piece(distance, c, side):
         device = chip_at(lax.rem(place + CHIPS - distance, CHIPS)) * 2 + side
@@ -325,7 +335,7 @@
 
 
 def correlate_kernel(
-    delays, me_ref, index_ref, g_ref, table_ref, out_ref, weights, cross, mixed, result, out_sem
+    me_ref, index_ref, g_ref, table_ref, out_ref, weights, cross, mixed, result, out_sem
 ):
     half = g_ref.shape[2]
     blocks, sources, receivers, _ = result.shape
@@ -347,8 +357,11 @@
         channel = lax.broadcasted_iota(jnp.int32, shape, axis) + h * half
         return jnp.where(channel == wanted, 1.0, 0.0).astype(jnp.bfloat16)
 
-    mine = lax.broadcasted_iota(jnp.int32, (receivers, half), 0) + me_ref[0] * receivers
-    pick = [chooser(h, mine, (receivers, half), 1) for h in range(2)]
+    slot = lax.broadcasted_iota(jnp.int32, (receivers, half), 0)
+    pick = []
+    for turn in range(QUAD):
+        mine = slot - lax.rem(slot, QUAD) + lax.rem(slot + QUAD - turn, QUAD) + me_ref[0] * receivers
+        pick.append([chooser(h, mine, (receivers, half), 1) for h in range(2)])
     width = 2 * SEGS * GROUP
     lane = lax.broadcasted_iota(jnp.int32, (GROUP, width), 1)
     same = lax.rem(lane, GROUP) == lax.broadcasted_iota(jnp.int32, (GROUP, width), 0)
@@ -357,7 +370,7 @@
         rows = jnp.zeros((receivers, width), jnp.float32)
         for h in range(2):
             rows = rows + lax.dot_general(
-                pick[h], spectra(group, h), (((1,), (1,)), ((), ())), preferred_element_type=jnp.float32
+                pick[group % QUAD][h], spectra(group, h), (((1,), (1,)), ((), ())), preferred_element_type=jnp.float32
             )
         turned = jnp.concatenate([-rows[:, width // 2 :], rows[:, : width // 2]], axis=1)
         weights[group, :, 0:GROUP, :] = (rows[:, None, :] * same).astype(jnp.bfloat16)
@@ -372,23 +385,42 @@
 
     def one_block(at, carry):
         wanted = index_ref[:, pl.ds(pl.multiple_of(at * sources, sources), sources)]
-        chosen_by = [chooser(h, wanted, (half, sources), 0) for h in range(2)]
-        part = 8
-        for group in range(GROUPS):
-            chosen = jnp.zeros((width, sources), jnp.float32)
-            for h in range(2):
-                chosen = chosen + jnp.dot(spectra(group, h), chosen_by[h], preferred_element_type=jnp.float32)
-            chosen = chosen.astype(jnp.bfloat16)
+        chosen_by = [chooser(h, wanted, (half, sources), 0).astype(jnp.float32).T for h in range(2)]
+        chosen_by = [one.astype(jnp.bfloat16) for one in chosen_by]
+        part = 2 * QUAD
+        quad_lanes = QUAD * 2 * GROUP
+        position = lax.rem(
+            lax.broadcasted_iota(jnp.int32, (sources, 2 * quad_lanes), 1) // (2 * GROUP), QUAD
+        )
+        for first in range(0, GROUPS, QUAD):
+            chosen = []
+            for group in range(first, first + QUAD):
+                rows = jnp.zeros((sources, width), jnp.float32)
+                for h in range(2):
+                    rows = rows + lax.dot_general(
+                        chosen_by[h], spectra(group, h), (((1,), (1,)), ((), ())),
+                        preferred_element_type=jnp.float32,
+                    )
+                chosen.append(rows.astype(jnp.bfloat16))
             for r in range(0, receivers, part):
-                block = weights[group, r : r + part].reshape(part * 2 * GROUP, width)
-                product = jnp.dot(block, chosen, preferred_element_type=jnp.float32)
-                cross[r : r + part, group * 2 * GROUP : (group + 1) * 2 * GROUP, :] = product.astype(
-                    jnp.bfloat16
-                ).reshape(part, 2 * GROUP, sources)
+                products = [
+                    lax.dot_general(
+                        chosen[turn], weights[first + turn, r : r + part].reshape(part * 2 * GROUP, width),
+                        (((1,), (1,)), ((), ())), preferred_element_type=jnp.float32,
+                    )
+                    for turn in range(QUAD)
+                ]
+                for a in range(QUAD):
+                    mixture = products[(QUAD - 1 - a) % QUAD]
+                    for j in range(QUAD - 1):
+                        mixture = jnp.where(position == j, products[(j - a) % QUAD], mixture)
+                    mixture = mixture.astype(jnp.bfloat16)
+                    lanes = slice(first * 2 * GROUP, (first + QUAD) * 2 * GROUP)
+                    cross[r + a, :, lanes] = mixture[:, :quad_lanes]
+                    cross[r + QUAD + a, :, lanes] = mixture[:, quad_lanes:]
         for r in range(receivers):
-            lagged = lax.dot_general(
-                cross[r], table_ref[delays], (((0,), (0,)), ((), ())), preferred_element_type=jnp.float32
-            )
+            delays = slice(r % QUAD * 2 * NF, (r % QUAD + 1) * 2 * NF)
+            lagged = jnp.dot(cross[r], table_ref[delays], preferred_element_type=jnp.float32)
             slot = r // side % 2
             for l in range(0, LAGS, 128):
                 mixed[slot, l // 128, pl.ds(r % side, sources, stride=side), :] = lagged[:, l : l + 128] * (
@@ -412,13 +444,9 @@
     half = channels // 2
     per_device = channel_mask.shape[0]
     me = lax.axis_index("chan")
-    spread = jnp.tile(channel_mask, channels // per_device)
-    mine = jnp.arange(channels, dtype=jnp.int32) // per_device == me
-    flags = jnp.where(mine, spread, 0).astype(jnp.bfloat16).reshape(2, half)
-    flags = jnp.pad(flags, ((0, FLAG_ROWS - 2), (0, 0)))
     block_table, tail_table = decimation_tables(raw_count)
     fourier = numpy_fourier()
-    tables = [block_table, tail_table, fourier[:, : NSEG // 2], fourier[:, NSEG // 2 :], numpy_delays()]
+    tables = [block_table, tail_table, fourier[:, : NSEG // 2], fourier[:, NSEG // 2 :]]
     tables = jnp.asarray(np.concatenate(tables))
     vmem = pl.BlockSpec(memory_space=pltpu.VMEM)
     hbm = pl.BlockSpec(memory_space=pltpu.HBM)
@@ -440,27 +468,27 @@
             collective_id=0, has_side_effects=True, vmem_limit_bytes=24 * MIB
         ),
         name="spectra",
-    )(recording, flags, tables)
+    )(recording, channel_mask.reshape(1, per_device), tables)
     sources = source_index.shape[0]
     block = 256
     receivers = per_device
     blocks = sources // block
     side = 16
     return pl.pallas_call(
-        functools.partial(correlate_kernel, table_rows(raw_count)[-1]),
+        correlate_kernel,
         out_shape=jax.ShapeDtypeStruct((sources, receivers, LAGS), bf16),
         in_specs=[pl.BlockSpec(memory_space=pltpu.SMEM), vmem, vmem, vmem],
         out_specs=hbm,
         scratch_shapes=[
             pltpu.VMEM((GROUPS, receivers, 2 * GROUP, 2 * SEGS * GROUP), bf16),
-            pltpu.VMEM((receivers, 2 * NF, block), bf16),
+            pltpu.VMEM((receivers, block, 2 * NF), bf16),
             pltpu.VMEM((2, LAGS // 128, block * side, 128), jnp.float32),
             pltpu.VMEM((blocks, block, receivers, LAGS), bf16),
             dma((blocks, receivers // side)),
         ],
         compiler_params=pltpu.CompilerParams(vmem_limit_bytes=44 * MIB),
         name="correlate",
-    )(me.reshape(1), source_index.reshape(1, sources), gathered, tables)
+    )(me.reshape(1), source_index.reshape(1, sources), gathered, jnp.asarray(numpy_delays()))
 
 
 def solution(mesh):

time: 56.6 us -> 54.5 us (0.963)
  Pallas kernels: 53.1 us -> 49.3 us
  local copies, waits for them, and re-layouts: 3.26 us -> 4.89 us
    pallas_call x1, Pallas kernels: 24.1 us -> 20.4 us  [fast_body(): pl.pallas_call(correlate_kernel, out_shape=jax.ShapeDtypeStruct((sources,...]
    unnamed x8 -> x10, local copies, waits for them, and re-layouts: 2.5 us -> 4.89 us
    another operation x2 -> x0, local copies, waits for them, and re-layouts: 0.75 us -> none  [fast_body(): spread = jnp.tile(channel_mask, channels // per_device)]
where the time goes in v2:
time: 54.5 us; the launch traced here: 54.3 us
  Pallas kernels  49.3 us (90%)
  local copies, waits for them, and re-layouts  4.89 us (9%)
    pallas_call x1, Pallas kernels, fast_body(): pl.pallas_call(spectra_kernel, out_shape=jax.ShapeDtypeStruct((2 * CHIPS,...  28.9 us
    pallas_call x1, Pallas kernels, fast_body(): pl.pallas_call(correlate_kernel, out_shape=jax.ShapeDtypeStruct((sources,...  20.4 us
    unnamed x10, local copies, waits for them, and re-layouts  4.89 us

profile of v2, /device:TPU:0, one launch (start us, length us, event | category | flops | bytes accessed | tf_op | source)
XLA Modules:
  0.0 54.3 jit_solution(15988274676579442276)
XLA Ops:
  0.0 0.0 copy-start
  0.0 1.2 %copy-done = bf16[512,1024]{1,0:T(8,128)(2,1)S(1)} copy-done((bf16[512,1024]{1,0:T(8,128)(2,1)S(1)}, bf16[512,1024]{1,0:T(8,128)(2,1)}, u32[]{:S(2)}) %copy-start) | copy-done | bytes 1048600
  1.2 0.0 copy-start.1
  1.2 1.2 %copy-done.1 = bf16[1920,256]{1,0:T(8,128)(2,1)S(1)} copy-done((bf16[1920,256]{1,0:T(8,128)(2,1)S(1)}, bf16[1920,256]{1,0:T(8,128)(2,1)}, u32[]{:S(2)}) %copy-start.1) | copy-done | bytes 983064
  2.4 0.0 copy-start.4
  2.4 0.7 %copy-done.4 = s32[32]{0:T(128)S(1)} copy-done((s32[32]{0:T(128)S(1)}, s32[32]{0:T(128)}, u32[]{:S(2)}) %copy-start.4) | copy-done | bytes 152
  3.1 28.9 %spectra.1.g_ref = bf16[16,400,256]{2,1,0:T(8,128)(2,1)S(1)} custom-call(bf16[512,1024]{1,0:T(8,128)(2,1)S(1)} %copy-done, s32[1,32]{1,0:T(1,128)S(1)} %bitcast.4, bf16[1920,256]{1,0:T(8,128)(2,1)S(1)} %copy-done.1), custom_call_target="tpu_custom_call" | custom-call | tf_op jit(solution)/shard_map/spectra/pallas_call | solution.py:456
  32.0 0.0 copy-start.2
  32.0 1.1 %copy-done.2 = bf16[1536,256]{1,0:T(8,128)(2,1)S(1)} copy-done((bf16[1536,256]{1,0:T(8,128)(2,1)S(1)}, bf16[1536,256]{1,0:T(8,128)(2,1)}, u32[]{:S(2)}) %copy-start.2) | copy-done | bytes 786456
  33.1 0.0 copy-start.3
  33.2 0.7 %copy-done.3 = s32[512]{0:T(512)S(1)} copy-done((s32[512]{0:T(512)S(1)}, s32[512]{0:T(512)}, u32[]{:S(2)}) %copy-start.3) | copy-done | bytes 2072
  33.8 20.4 %correlate.1 = bf16[512,32,256]{2,1,0:T(8,128)(2,1)} custom-call(s32[1]{0:T(128)} %bitcast.me_ref, s32[1,512]{1,0:T(1,128)S(1)} %bitcast.3, bf16[16,400,256]{2,1,0:T(8,128)(2,1)S(1)} %spectra.1.g_ref, bf16[1536,256]{1,0:T(8,128)(2,1)S(1)} %copy-done.2), custom_call_target="tpu_custom_call" | custom-call | tf_op jit(solution)/shard_map/correlate/pallas_call | solution.py:477
Async XLA Ops:
  0.0 1.2 %copy-start = (bf16[512,1024]{1,0:T(8,128)(2,1)S(1)}, bf16[512,1024]{1,0:T(8,128)(2,1)}, u32[]{:S(2)}) copy-start(bf16[512,1024]{1,0:T(8,128)(2,1)} %x_ref.1) | copy-start | bytes 3145732
  1.2 1.2 %copy-start.1 = (bf16[1920,256]{1,0:T(8,128)(2,1)S(1)}, bf16[1920,256]{1,0:T(8,128)(2,1)}, u32[]{:S(2)}) copy-start(bf16[1920,256]{1,0:T(8,128)(2,1)} %constant.8.clone.table_ref) | copy-start | bytes 2949124
  2.4 0.7 %copy-start.4 = (s32[32]{0:T(128)S(1)}, s32[32]{0:T(128)}, u32[]{:S(2)}) copy-start(s32[32]{0:T(128)} %param.7) | copy-start | bytes 388
  32.0 1.1 %copy-start.2 = (bf16[1536,256]{1,0:T(8,128)(2,1)S(1)}, bf16[1536,256]{1,0:T(8,128)(2,1)}, u32[]{:S(2)}) copy-start(bf16[1536,256]{1,0:T(8,128)(2,1)} %constant.9.clone.table_ref) | copy-start | bytes 2359300
  33.1 0.7 %copy-start.3 = (s32[512]{0:T(512)S(1)}, s32[512]{0:T(512)}, u32[]{:S(2)}) copy-start(s32[512]{0:T(512)} %param.6) | copy-start | bytes 6148

commit v3 on v2

--- a/solution.py
+++ b/solution.py
@@ -1,3 +1,4 @@
+import functools
 import math
 
 import jax
@@ -168,14 +169,12 @@
     frequency = FBASE + np.arange(NF)[:, None]
     delays = np.arange(LAGS)[None, :] - LAGS // 2
     angles = 2.0 * np.pi * (frequency * delays % NSEG) / NSEG
-    pair = np.stack([np.cos(angles), -np.sin(angles)]).reshape(2, GROUPS, GROUP, LAGS).transpose(1, 0, 2, 3)
-    slot = np.arange(GROUPS)
-    order = [slot // QUAD * QUAD + (slot - a) % QUAD for a in range(QUAD)]
-    return np.concatenate([pair[at].reshape(2 * NF, LAGS) for at in order]).astype(ml_dtypes.bfloat16)
+    pair = np.stack([np.cos(angles), -np.sin(angles)]).reshape(2, GROUPS, GROUP, LAGS)
+    return pair.transpose(1, 0, 2, 3).reshape(2 * NF, LAGS).astype(ml_dtypes.bfloat16)
 
 
 def table_rows(raw_count):
-    ends = np.cumsum([0, raw_count, TAIL, 2 * NF, 2 * NF])
+    ends = np.cumsum([0, raw_count, TAIL, 2 * NF, 2 * NF, 2 * NF])
     return [slice(int(a), int(b)) for a, b in zip(ends[:-1], ends[1:])]
 
 
@@ -260,7 +259,7 @@
     def product(a, b):
         return jnp.dot(a, b, preferred_element_type=jnp.float32)
 
-    block, tail, before, after = table_rows(raw_count)
+    block, tail, before, after, _ = table_rows(raw_count)
     first = product(xs[0], table_ref[block]) + product(halo[...], table_ref[tail])
     second = product(xs[1], table_ref[block]) + product(xs[0, :, raw_count - TAIL :], table_ref[tail])
 
@@ -335,11 +334,21 @@
 
 
 def correlate_kernel(
-    me_ref, index_ref, g_ref, table_ref, out_ref, weights, cross, mixed, result, out_sem
+    delays_at, me_ref, index_ref, g_ref, table_ref, out_ref, weights, cross, lagged, turned_delays, result, out_sem
 ):
     half = g_ref.shape[2]
     blocks, sources, receivers, _ = result.shape
-    side = mixed.shape[2] // sources
+    side = 16
+    chunk = 2 * GROUP
+    for a in range(QUAD):
+        for j in range(GROUPS):
+            group = j // QUAD * QUAD + (j - a) % QUAD
+            start = delays_at + group * chunk
+            turned_delays[a, j * chunk : (j + 1) * chunk, :] = table_ref[start : start + chunk, :]
+    to_row = lax.broadcasted_iota(jnp.int32, (side * side, side * side), 0)
+    from_row = lax.broadcasted_iota(jnp.int32, (side * side, side * side), 1)
+    swap = from_row == lax.rem(to_row, side) * side + to_row // side
+    swap = jnp.where(swap, 1.0, 0.0).astype(jnp.bfloat16)
     flags = g_ref[0, 2 * NF : ROWS, :].astype(jnp.float32)
     for device in range(1, 2 * CHIPS):
         flags = flags + g_ref[device, 2 * NF : ROWS, :].astype(jnp.float32)
@@ -389,9 +398,9 @@
         chosen_by = [one.astype(jnp.bfloat16) for one in chosen_by]
         part = 2 * QUAD
         quad_lanes = QUAD * 2 * GROUP
-        position = lax.rem(
-            lax.broadcasted_iota(jnp.int32, (sources, 2 * quad_lanes), 1) // (2 * GROUP), QUAD
-        )
+        strip = 64
+        position = lax.rem(lax.broadcasted_iota(jnp.int32, (strip, 2 * quad_lanes), 1) // (2 * GROUP), QUAD)
+        position = position.astype(jnp.float32).astype(jnp.bfloat16)
         for first in range(0, GROUPS, QUAD):
             chosen = []
             for group in range(first, first + QUAD):
@@ -407,30 +416,28 @@
                     lax.dot_general(
                         chosen[turn], weights[first + turn, r : r + part].reshape(part * 2 * GROUP, width),
                         (((1,), (1,)), ((), ())), preferred_element_type=jnp.float32,
-                    )
+                    ).astype(jnp.bfloat16)
                     for turn in range(QUAD)
                 ]
-                for a in range(QUAD):
-                    mixture = products[(QUAD - 1 - a) % QUAD]
-                    for j in range(QUAD - 1):
-                        mixture = jnp.where(position == j, products[(j - a) % QUAD], mixture)
-                    mixture = mixture.astype(jnp.bfloat16)
-                    lanes = slice(first * 2 * GROUP, (first + QUAD) * 2 * GROUP)
-                    cross[r + a, :, lanes] = mixture[:, :quad_lanes]
-                    cross[r + QUAD + a, :, lanes] = mixture[:, quad_lanes:]
-        for r in range(receivers):
-            delays = slice(r % QUAD * 2 * NF, (r % QUAD + 1) * 2 * NF)
-            lagged = jnp.dot(cross[r], table_ref[delays], preferred_element_type=jnp.float32)
-            slot = r // side % 2
-            for l in range(0, LAGS, 128):
-                mixed[slot, l // 128, pl.ds(r % side, sources, stride=side), :] = lagged[:, l : l + 128] * (
-                    1.0 / math.sqrt(SEGS * NF)
-                )
-            if r % side == side - 1:
-                for l in range(0, LAGS, 128):
-                    done = mixed[slot, l // 128].reshape(sources, side, 128).astype(jnp.bfloat16)
-                    result[at, :, r - side + 1 : r + 1, l : l + 128] = done
-                write(at, r // side).start()
+                lanes = slice(first * 2 * GROUP, (first + QUAD) * 2 * GROUP)
+                for top in range(0, sources, strip):
+                    rows = slice(top, top + strip)
+                    strips = [product[rows] for product in products]
+                    for a in range(QUAD):
+                        mixture = strips[(QUAD - 1 - a) % QUAD]
+                        for j in range(QUAD - 1):
+                            mixture = jnp.where(position == j, strips[(j - a) % QUAD], mixture)
+                        cross[r + a, rows, lanes] = mixture[:, :quad_lanes]
+                        cross[r + QUAD + a, rows, lanes] = mixture[:, quad_lanes:]
+        for part in range(0, receivers, side):
+            for r in range(part, part + side):
+                lags = jnp.dot(cross[r], turned_delays[r % QUAD], preferred_element_type=jnp.float32)
+                lagged[r] = (lags * (1.0 / math.sqrt(SEGS * NF))).astype(jnp.bfloat16)
+            for top in range(0, sources, side):
+                tile = lagged[part : part + side, top : top + side, :].reshape(side * side, LAGS)
+                tile = jnp.dot(swap, tile, preferred_element_type=jnp.float32).astype(jnp.bfloat16)
+                result[at, top : top + side, part : part + side, :] = tile.reshape(side, side, LAGS)
+            write(at, part // side).start()
         return carry
 
     lax.fori_loop(0, blocks, one_block, 0)
@@ -446,7 +453,7 @@
     me = lax.axis_index("chan")
     block_table, tail_table = decimation_tables(raw_count)
     fourier = numpy_fourier()
-    tables = [block_table, tail_table, fourier[:, : NSEG // 2], fourier[:, NSEG // 2 :]]
+    tables = [block_table, tail_table, fourier[:, : NSEG // 2], fourier[:, NSEG // 2 :], numpy_delays()]
     tables = jnp.asarray(np.concatenate(tables))
     vmem = pl.BlockSpec(memory_space=pltpu.VMEM)
     hbm = pl.BlockSpec(memory_space=pltpu.HBM)
@@ -475,20 +482,21 @@
     blocks = sources // block
     side = 16
     return pl.pallas_call(
-        correlate_kernel,
+        functools.partial(correlate_kernel, table_rows(raw_count)[-1].start),
         out_shape=jax.ShapeDtypeStruct((sources, receivers, LAGS), bf16),
         in_specs=[pl.BlockSpec(memory_space=pltpu.SMEM), vmem, vmem, vmem],
         out_specs=hbm,
         scratch_shapes=[
             pltpu.VMEM((GROUPS, receivers, 2 * GROUP, 2 * SEGS * GROUP), bf16),
             pltpu.VMEM((receivers, block, 2 * NF), bf16),
-            pltpu.VMEM((2, LAGS // 128, block * side, 128), jnp.float32),
+            pltpu.VMEM((receivers, block, LAGS), bf16),
+            pltpu.VMEM((QUAD, 2 * NF, LAGS), bf16),
             pltpu.VMEM((blocks, block, receivers, LAGS), bf16),
             dma((blocks, receivers // side)),
         ],
         compiler_params=pltpu.CompilerParams(vmem_limit_bytes=44 * MIB),
         name="correlate",
-    )(me.reshape(1), source_index.reshape(1, sources), gathered, jnp.asarray(numpy_delays()))
+    )(me.reshape(1), source_index.reshape(1, sources), gathered, tables)
 
 
 def solution(mesh):

time: 54.5 us -> 48.6 us (0.89)
  Pallas kernels: 49.3 us -> 45.3 us
  local copies, waits for them, and re-layouts: 4.89 us -> 3.17 us
    pallas_call x1, Pallas kernels: 20.4 us -> 16.3 us  [fast_body(): pl.pallas_call(functools.partial(correlate_kernel, table_rows(raw_count)[...]
    unnamed x10, local copies, waits for them, and re-layouts: 4.89 us -> 3.17 us
where the time goes in v3:
time: 48.6 us; the launch traced here: 48.5 us
  Pallas kernels  45.3 us (93%)
  local copies, waits for them, and re-layouts  3.17 us (7%)
    pallas_call x1, Pallas kernels, fast_body(): pl.pallas_call(spectra_kernel, out_shape=jax.ShapeDtypeStruct((2 * CHIPS,...  28.9 us
    pallas_call x1, Pallas kernels, fast_body(): pl.pallas_call(functools.partial(correlate_kernel, table_rows(raw_count)[...  16.3 us
    unnamed x10, local copies, waits for them, and re-layouts  3.17 us

profile of v3, /device:TPU:0, one launch (start us, length us, event | category | flops | bytes accessed | tf_op | source)
XLA Modules:
  0.0 48.5 jit_solution(93863401588621563)
XLA Ops:
  0.0 0.0 copy-start.3
  0.0 0.0 copy-start
  0.0 1.3 %copy-done = bf16[2304,256]{1,0:T(8,128)(2,1)S(1)} copy-done((bf16[2304,256]{1,0:T(8,128)(2,1)S(1)}, bf16[2304,256]{1,0:T(8,128)(2,1)}, u32[]{:S(2)}) %copy-start) | copy-done | bytes 1179672
  1.3 0.0 copy-start.2
  1.3 1.2 %copy-done.2 = bf16[512,1024]{1,0:T(8,128)(2,1)S(1)} copy-done((bf16[512,1024]{1,0:T(8,128)(2,1)S(1)}, bf16[512,1024]{1,0:T(8,128)(2,1)}, u32[]{:S(2)}) %copy-start.2) | copy-done | bytes 1048600
  2.5 0.0 copy-start.4
  2.5 0.7 %copy-done.4 = s32[32]{0:T(128)S(1)} copy-done((s32[32]{0:T(128)S(1)}, s32[32]{0:T(128)}, u32[]{:S(2)}) %copy-start.4) | copy-done | bytes 152
  3.2 0.0 copy-start.1
  3.2 28.9 %spectra.1.g_ref = bf16[16,400,256]{2,1,0:T(8,128)(2,1)S(1)} custom-call(bf16[512,1024]{1,0:T(8,128)(2,1)S(1)} %copy-done.2, s32[1,32]{1,0:T(1,128)S(1)} %bitcast.4, bf16[2304,256]{1,0:T(8,128)(2,1)S(1)} %copy-done), custom_call_target="tpu_custom_call" | custom-call | tf_op jit(solution)/shard_map/spectra/pallas_call | solution.py:463
  32.1 0.0 copy-done.3
  32.1 0.0 copy-done.1
  32.1 16.3 %correlate.1 = bf16[512,32,256]{2,1,0:T(8,128)(2,1)} custom-call(s32[1]{0:T(128)} %bitcast.me_ref, s32[1,512]{1,0:T(1,128)S(1)} %bitcast.3, bf16[16,400,256]{2,1,0:T(8,128)(2,1)S(1)} %spectra.1.g_ref, bf16[2304,256]{1,0:T(8,128)(2,1)S(1)} %copy-done.1), custom_call_target="tpu_custom_call" | custom-call | tf_op jit(solution)/shard_map/correlate/pallas_call | solution.py:484
Async XLA Ops:
  0.0 32.1 %copy-start.3 = (s32[512]{0:T(512)S(1)}, s32[512]{0:T(512)}, u32[]{:S(2)}) copy-start(s32[512]{0:T(512)} %param.5) | copy-start | bytes 6148
  0.0 1.3 %copy-start = (bf16[2304,256]{1,0:T(8,128)(2,1)S(1)}, bf16[2304,256]{1,0:T(8,128)(2,1)}, u32[]{:S(2)}) copy-start(bf16[2304,256]{1,0:T(8,128)(2,1)} %constant.6.clone.table_ref) | copy-start | bytes 3538948
  1.3 1.2 %copy-start.2 = (bf16[512,1024]{1,0:T(8,128)(2,1)S(1)}, bf16[512,1024]{1,0:T(8,128)(2,1)}, u32[]{:S(2)}) copy-start(bf16[512,1024]{1,0:T(8,128)(2,1)} %x_ref.1) | copy-start | bytes 3145732
  2.5 0.7 %copy-start.4 = (s32[32]{0:T(128)S(1)}, s32[32]{0:T(128)}, u32[]{:S(2)}) copy-start(s32[32]{0:T(128)} %param.6) | copy-start | bytes 388
  3.2 29.0 %copy-start.1 = (bf16[2304,256]{1,0:T(8,128)(2,1)S(1)}, bf16[2304,256]{1,0:T(8,128)(2,1)}, u32[]{:S(2)}) copy-start(bf16[2304,256]{1,0:T(8,128)(2,1)} %constant.6.clone.table_ref) | copy-start | bytes 3538948
